TPU v7x, 32 devices: a whole 2x2x4 slice. The times are simulated.
32 devices in a mesh: fsdp: 16 (over z, y, core), ctx: 2 (over x).
Axes of the slice: x: 2, y: 2, z: 4, core: 2. Of those that a mesh axis runs over, the one named last changes fastest.
Arguments:
- queries: bfloat16 [16, 256, 1536], P('fsdp', 'ctx'), may hold values from -1.6953125 to 1.6953125
- key_states: bfloat16 [16, 256, 1536], P('fsdp', 'ctx'), may hold values from -1.6953125 to 1.6953125
- value_states: bfloat16 [16, 256, 1536], P('fsdp', 'ctx'), may hold values from -6 to 6
- attn_out: bfloat16 [16, 256, 1536], P('fsdp', 'ctx'), may hold values from -6 to 6
- log_norm: bfloat16 [16, 256, 12], P('fsdp', 'ctx'), may hold values from 3 to 4.5
- out_grad: bfloat16 [16, 256, 3072], P('fsdp', 'ctx'), may hold values from -6 to 6
- proj_weight: bfloat16 [1536, 3072], P('fsdp', 'ctx'), may hold values from -0.109375 to 0.109375
- tile_mask: int32 [16, 12, 4, 4], P('fsdp'), may hold values from 0 to 1, as said below
Outputs:
- grad_query: bfloat16 [16, 256, 1536], P('fsdp', 'ctx')
- grad_key: bfloat16 [16, 256, 1536], P('fsdp', 'ctx')
- grad_value: bfloat16 [16, 256, 1536], P('fsdp', 'ctx')
Inputs may be any that keep to these rules, and one draw needn't show every extreme that they name: tile_mask[c, h, i, j] = 1 lets the query tokens of tile i attend to the key tokens of tile j in head h; a tile is 64 consecutive tokens; every tile attends to itself.
All inputs are finite; a program needn't handle non-finite values.
Results may differ from a plain program's by a relative error of at most 0.014.
Values may be sent and summed in bfloat16 or wider, within the bound.
A program may use at most 64 MiB of HBM per device.

v0:
```python
import jax
import jax.numpy as jnp
from jax import lax
from jax.sharding import PartitionSpec as P

H = 12
HD = 128
TILE = 64


def round_trip(array):
    return lax.optimization_barrier(array.astype(jnp.bfloat16)).astype(jnp.float32)


def tile_onehot(row_count, tile_count):
    tile_ids = jnp.arange(row_count, dtype=jnp.int32) // TILE
    return (tile_ids[:, None] == jnp.arange(tile_count, dtype=jnp.int32)[None, :]).astype(
        jnp.float32
    )


def score_terms(
    query_head_rows, gradient_by_head, norm_rows, dots_rows, key_head_rows, value_head_rows, allowed
):
    score_scale = HD ** (-0.5)
    scores = (
        jnp.einsum(
            "vgl,ygl->gvy", query_head_rows, key_head_rows, preferred_element_type=jnp.float32
        )
        * score_scale
    )
    attn_prob = jnp.exp(scores - norm_rows.T[:, :, None]) * allowed
    prob_grad = jnp.einsum(
        "vgl,ygl->gvy", gradient_by_head, value_head_rows, preferred_element_type=jnp.float32
    )
    score_grad = attn_prob * (prob_grad - dots_rows.T[:, :, None])
    return (attn_prob.astype(jnp.bfloat16), score_grad.astype(jnp.bfloat16))


def local(queries, key_states, value_states, attn_out, log_norm, out_grad, proj_weight, tile_mask):
    ctx_count = lax.axis_size("ctx")
    ctx_index = lax.axis_index("ctx")
    tok_rows = queries.shape[1]
    hid_width = queries.shape[2]
    score_scale = HD ** (-0.5)
    tile_table = tile_mask[0]
    tile_count = tile_table.shape[1]
    own_count = tok_rows // TILE
    grad_slab = lax.all_to_all(out_grad[0], "ctx", split_axis=1, concat_axis=0, tiled=True)
    product = lax.dot_general(
        grad_slab,
        lax.all_gather(proj_weight, "fsdp", axis=0, tiled=True),
        (((1,), (1,)), ((), ())),
        preferred_element_type=jnp.float32,
    )
    partial_value = product.astype(jnp.bfloat16)
    arrived = lax.all_to_all(
        partial_value.reshape(ctx_count, tok_rows, hid_width),
        "ctx",
        split_axis=0,
        concat_axis=0,
        tiled=True,
    )
    attn_grad = jnp.sum(arrived.astype(jnp.float32), axis=0).astype(jnp.bfloat16)
    query_head_rows = queries[0].reshape(tok_rows, H, HD)
    gradient_by_head = attn_grad.reshape(tok_rows, H, HD)
    out_heads = attn_out[0].reshape(tok_rows, H, HD)
    dots_round = jnp.sum(
        gradient_by_head.astype(jnp.float32) * out_heads.astype(jnp.float32), axis=-1
    ).astype(jnp.bfloat16)
    own_rows = jnp.repeat(
        lax.dynamic_slice_in_dim(tile_table, ctx_index * own_count, own_count, 1).astype(
            jnp.float32
        ),
        TILE,
        axis=1,
    )
    norm_rows = log_norm[0].astype(jnp.float32)
    dots_rows = lax.optimization_barrier(dots_round).astype(jnp.float32)
    key_rows = lax.all_gather(key_states[0], "ctx", axis=0, tiled=True)
    value_rows = lax.all_gather(value_states[0], "ctx", axis=0, tiled=True)
    piece_rows = key_rows.shape[0]
    sub_rows = min(piece_rows, tok_rows)
    blocks_in = piece_rows // sub_rows
    key_block = key_rows.reshape(piece_rows, H, HD)
    value_block = value_rows.reshape(piece_rows, H, HD)
    allowed = jnp.einsum("htn,mn->htm", own_rows, tile_onehot(piece_rows, tile_count))
    probability_per_round, gradient_per_round = score_terms(
        query_head_rows, gradient_by_head, norm_rows, dots_rows, key_block, value_block, allowed
    )
    value_term = jnp.einsum(
        "bve,vbt->ebt", probability_per_round, gradient_by_head, preferred_element_type=jnp.float32
    )
    key_term = (
        jnp.einsum(
            "bve,vbt->ebt", gradient_per_round, query_head_rows, preferred_element_type=jnp.float32
        )
        * score_scale
    )
    query_term = (
        jnp.einsum(
            "hmbn,bnhd->bmhd",
            gradient_per_round.reshape(H, tok_rows, blocks_in, sub_rows),
            key_block.reshape(blocks_in, sub_rows, H, HD),
            preferred_element_type=jnp.float32,
        )
        * score_scale
    )
    part_slots = query_term.reshape(blocks_in, tok_rows, hid_width)
    key_total = key_term.reshape(piece_rows, hid_width)
    value_total = value_term.reshape(piece_rows, hid_width)
    part_slots, key_total, value_total = (part_slots, key_total, value_total)
    grad_query = jnp.sum(round_trip(part_slots), axis=0).astype(jnp.bfloat16)
    key_parts, value_parts = (
        lax.all_to_all(
            key_total.astype(jnp.bfloat16).reshape(ctx_count, tok_rows, hid_width),
            "ctx",
            split_axis=0,
            concat_axis=0,
            tiled=True,
        ),
        lax.all_to_all(
            value_total.astype(jnp.bfloat16).reshape(ctx_count, tok_rows, hid_width),
            "ctx",
            split_axis=0,
            concat_axis=0,
            tiled=True,
        ),
    )
    grad_key = jnp.sum(key_parts.astype(jnp.float32), axis=0).astype(jnp.bfloat16)
    grad_value = jnp.sum(value_parts.astype(jnp.float32), axis=0).astype(jnp.bfloat16)
    return (grad_query[None], grad_key[None], grad_value[None])


def solution(mesh):
    placed = (
        P("fsdp", "ctx", None),
        P("fsdp", "ctx", None),
        P("fsdp", "ctx", None),
        P("fsdp", "ctx", None),
        P("fsdp", "ctx", None),
        P("fsdp", "ctx", None),
        P("fsdp", "ctx"),
        P("fsdp", None, None, None),
    )
    return jax.shard_map(
        local,
        mesh=mesh,
        in_specs=placed,
        out_specs=(P("fsdp", "ctx", None), P("fsdp", "ctx", None), P("fsdp", "ctx", None)),
        check_vma=False,
    )
```

profile of v0, /device:TPU:0, one launch (start us, length us, event | category | flops | bytes accessed | tf_op | source)
XLA Modules:
  0.0 145.3 jit_solution(11304520714895516821)
XLA Ops:
  7.2 0.7 all-gather.4.cloned.1.call-update
  7.9 2.3 %copy.78 = bf16[1,128,3072]{1,2,0:T(8,128)(2,1)} copy(bf16[1,128,3072]{2,1,0:T(8,128)(2,1)} %param.13) | data formatting | bytes 1572864 | tf_op args[5]
  10.2 4.3 %all-to-all-start = ((bf16[128,2,1536]{0,2,1:T(8,128)(2,1)}), bf16[128,2,1536]{0,2,1:T(8,128)(2,1)S(1)}, u32[]{:S(2)}, u32[]{:S(2)}) async-start(bf16[128,2,1536]{0,2,1:T(8,128)(2,1)} %bitcast.6), calls=%async_computation | async-start | bytes 1572864 | tf_op jit(solution)/shard_map/all_to_all | solution.py:49
  14.8 19.8 %all-gather = bf16[1,256,1536]{1,2,0:T(8,128)(2,1)S(1)} all-gather(bf16[1,128,1536]{1,2,0:T(8,128)(2,1)S(1)} %copy.74), channel_id=2, replica_groups=mesh['fsdp'=16,'ctx'=2] {'ctx'}, dimensions={1}, use_global_device_ids=true | all-gather | bytes 1179648 | tf_op jit(solution)/shard_map/all_gather | solution.py:80
  35.2 1.6 %fusion.8 = f32[12,128,256]{2,1,0:T(8,128)} fusion(bf16[12,128,4]{1,2,0:T(4,128)(2,1)S(1)} %reshape.60, s32[256]{0:T(256)S(1)} %and_select_fusion), kind=kOutput, calls=%fused_computation.19 | convolution fusion | flops 3146752 | bytes 1586176 | tf_op jit(solution)/shard_map/htn,mn->htm/dot_general | solution.py:87
  37.1 29.4 %all-gather.4.cloned.1.call-done = bf16[1536,1536]{1,0:T(8,128)(2,1)} async-done(((bf16[96,1536]{1,0:T(8,128)(2,1)}), bf16[1536,1536]{1,0:T(8,128)(2,1)}) %all-gather.4.cloned.1.call-update) | async-done | bytes 4718608 | tf_op jit(solution)/shard_map/all_gather | solution.py:52
  66.5 4.6 %convolution_convert_fusion = bf16[256,1536]{1,0:T(8,128)(2,1)} fusion(bf16[256,1536]{1,0:T(8,128)(2,1)S(1)} %bitcast.69, bf16[1536,1536]{1,0:T(8,128)(2,1)} %all-gather.4.cloned.1.call-done), kind=kOutput, calls=%fused_computation | convolution fusion | flops 1208352768 | bytes 6291456 | tf_op jit(solution)/shard_map/dot_general | solution.py:50
  71.1 4.4 %all-to-all-start.1 = ((bf16[2,128,1536]{2,1,0:T(8,128)(2,1)}), bf16[2,128,1536]{2,1,0:T(8,128)(2,1)}, u32[]{:S(2)}, u32[]{:S(2)}) async-start(bf16[2,128,1536]{2,1,0:T(8,128)(2,1)} %bitcast.9), calls=%async_computation.1 | async-start | bytes 1572864 | tf_op jit(solution)/shard_map/all_to_all | solution.py:57
  75.5 20.0 %all-gather.1 = bf16[1,256,1536]{1,2,0:T(8,128)(2,1)} all-gather(bf16[1,128,1536]{1,2,0:T(8,128)(2,1)S(1)} %copy.81), channel_id=3, replica_groups=mesh['fsdp'=16,'ctx'=2] {'ctx'}, dimensions={1}, use_global_device_ids=true | all-gather | bytes 1179648 | tf_op jit(solution)/shard_map/all_gather | solution.py:81
  96.0 1.9 %exponential_multiply_fusion = f32[12,128,256]{2,1,0:T(8,128)S(1)} fusion(f32[12,128,256]{2,1,0:T(8,128)} %fusion.8, bf16[128,12,128]{0,2,1:T(8,128)(2,1)S(1)} %bitcast.61, bf16[256,12,128]{0,2,1:T(8,128)(2,1)S(1)} %bitcast.57, f32[12,128]{1,0:T(8,128)S(1)} %convert_bitcast_fusion), kind=kOutput, calls=%fused_computation.4 | convolution fusion | flops 101842944 | bytes 4331520 | tf_op jit(solution)/shard_map/vgl,ygl->gvy/dot_general | solution.py:27
  98.0 2.1 %reduce_sum.57 = bf16[128,1536]{1,0:T(8,128)(2,1)} reduce(bf16[2,128,1536]{2,1,0:T(8,128)(2,1)} %all-to-all-done.1, bf16[]{:T(256)} %constant.37.clone.1), dimensions={0}, to_apply=%region_0.0 | reduce | flops 196608 | bytes 1179650 | tf_op jit(solution)/shard_map/reduce_sum | solution.py:64
  100.1 1.2 copy.80
  101.4 1.6 %multiply_convert_fusion.2 = bf16[12,128,256]{2,1,0:T(8,128)(2,1)S(1)} fusion(f32[12,128,256]{2,1,0:T(8,128)S(1)} %exponential_multiply_fusion, bf16[128,12,128]{0,2,1:T(8,128)(2,1)S(1)} %bitcast.59, bf16[256,12,128]{0,2,1:T(8,128)(2,1)} %bitcast.63, f32[12,128]{1,0:T(8,128)S(1)} %convert_bitcast_fusion.1), kind=kOutput, calls=%fused_computation.3 | convolution fusion | flops 101842944 | bytes 3545088 | tf_op jit(solution)/shard_map/vgl,ygl->gvy/dot_general | solution.py:33
  103.0 0.9 copy-done
  103.9 1.3 fusion.1
  105.2 1.4 copy.89
  106.6 1.1 convert_element_type.84
  107.7 2.1 %copy.90 = bf16[2,128,1536]{1,2,0:T(8,128)(2,1)} copy(bf16[2,128,1536]{1,0,2:T(2,128)(2,1)} %convert_element_type.84) | data formatting | bytes 1572864 | tf_op jit(solution)/shard_map/convert_element_type | solution.py:116
  109.9 3.5 %all-to-all-start.2 = ((bf16[2,128,1536]{1,2,0:T(8,128)(2,1)}), bf16[2,128,1536]{1,2,0:T(8,128)(2,1)S(1)}, u32[]{:S(2)}, u32[]{:S(2)}) async-start(bf16[2,128,1536]{1,2,0:T(8,128)(2,1)} %copy.90), calls=%async_computation.2 | async-start | bytes 1572864 | tf_op jit(solution)/shard_map/all_to_all | solution.py:115
  113.4 1.3 fusion
  114.7 2.0 %convert_element_type.88 = bf16[2,128,1536]{1,0,2:T(2,128)(2,1)S(1)} reshape(bf16[256,12,128]{0,2,1:T(8,128)(2,1)} %fusion) | data formatting | bytes 1572864 | tf_op jit(solution)/shard_map/convert_element_type | solution.py:123
  116.7 1.0 copy.92
  117.7 6.3 %all-to-all-done.2 = bf16[2,128,1536]{1,2,0:T(8,128)(2,1)S(1)} async-done(((bf16[2,128,1536]{1,2,0:T(8,128)(2,1)}), bf16[2,128,1536]{1,2,0:T(8,128)(2,1)S(1)}, u32[]{:S(2)}, u32[]{:S(2)}) %all-to-all-start.2) | async-done | bytes 786464 | tf_op jit(solution)/shard_map/all_to_all | solution.py:115
  124.0 3.5 %all-to-all-start.3 = ((bf16[2,128,1536]{1,2,0:T(8,128)(2,1)}), bf16[2,128,1536]{1,2,0:T(8,128)(2,1)S(1)}, u32[]{:S(2)}, u32[]{:S(2)}) async-start(bf16[2,128,1536]{1,2,0:T(8,128)(2,1)} %copy.92), calls=%async_computation.3 | async-start | bytes 1572864 | tf_op jit(solution)/shard_map/all_to_all | solution.py:122
  127.5 1.1 reshape_reshape.3
  128.6 2.7 %multiply_convert_fusion.1 = bf16[2,12,128,128]{2,3,1,0:T(8,128)(2,1)} fusion(bf16[2,128,12,128]{1,0,3,2:T(2,128)(2,1)} %reshape_reshape.3, bf16[12,128,256]{2,1,0:T(8,128)(2,1)S(1)} %copy-done.1), kind=kOutput, calls=%fused_computation.2 | convolution fusion | flops 101449728 | bytes 2359296 | tf_op jit(solution)/shard_map/hmbn,bnhd->bmhd/dot_general | solution.py:101
  131.3 1.5 %reduce_sum.59 = bf16[128,1536]{0,1:T(8,128)(2,1)S(1)} reduce(bf16[2,128,1536]{1,2,0:T(8,128)(2,1)} %bitcast.70, bf16[]{:T(256)} %constant.37.clone.1), dimensions={0}, to_apply=%region_2.3 | reduce | flops 196608 | bytes 1179650 | tf_op jit(solution)/shard_map/reduce_sum | solution.py:113
  132.7 0.9 copy.94
  133.7 0.4 reduce_sum.60
  134.0 0.9 copy.95
  134.9 2.2 %all-to-all-done.3 = bf16[2,128,1536]{1,2,0:T(8,128)(2,1)S(1)} async-done(((bf16[2,128,1536]{1,2,0:T(8,128)(2,1)}), bf16[2,128,1536]{1,2,0:T(8,128)(2,1)S(1)}, u32[]{:S(2)}, u32[]{:S(2)}) %all-to-all-start.3) | async-done | bytes 786464 | tf_op jit(solution)/shard_map/all_to_all | solution.py:122
  137.5 0.9 copy.96
  (32 shorter events, 2.1 us)
Async XLA Ops:
  7.2 59.3 %all-gather.4.cloned.1.call-start = ((), (), s32[]{:S(2)}) async-start(), calls=%async_computation.4 | async-start | bytes 5013504 | tf_op jit(solution)/shard_map/all_gather | solution.py:52
  7.9 6.7 %copy-start.2 = (bf16[1,128,1536]{2,1,0:T(8,128)(2,1)S(1)}, bf16[1,128,1536]{2,1,0:T(8,128)(2,1)}, u32[]{:S(2)}) copy-start(bf16[1,128,1536]{2,1,0:T(8,128)(2,1)} %param.9) | copy-start | bytes 1179652
  10.2 24.4 %copy-start.6 = (bf16[1,128,12]{1,2,0:T(8,128)(2,1)S(1)}, bf16[1,128,12]{1,2,0:T(8,128)(2,1)}, u32[]{:S(2)}) copy-start(bf16[1,128,12]{1,2,0:T(8,128)(2,1)} %param.12) | copy-start | bytes 9220
  10.2 24.4 %copy-start.7 = (s32[1,12,4,4]{1,3,2,0:T(4,128)S(1)}, s32[1,12,4,4]{1,3,2,0:T(4,128)}, u32[]{:S(2)}) copy-start(s32[1,12,4,4]{1,3,2,0:T(4,128)} %param.15) | copy-start | bytes 2308
  10.2 24.7 %copy-start.3 = (bf16[1,128,1536]{2,1,0:T(8,128)(2,1)S(1)}, bf16[1,128,1536]{2,1,0:T(8,128)(2,1)}, u32[]{:S(2)}) copy-start(bf16[1,128,1536]{2,1,0:T(8,128)(2,1)} %param.10) | copy-start | bytes 1179652
  10.2 26.6 %all-to-all-start = ((bf16[128,2,1536]{0,2,1:T(8,128)(2,1)}), bf16[128,2,1536]{0,2,1:T(8,128)(2,1)S(1)}, u32[]{:S(2)}, u32[]{:S(2)}) async-start(bf16[128,2,1536]{0,2,1:T(8,128)(2,1)} %bitcast.6), calls=%async_computation | async-start | bytes 1572864 | tf_op jit(solution)/shard_map/all_to_all | solution.py:49
  71.1 24.5 %copy-start.4 = (bf16[1,128,1536]{2,1,0:T(8,128)(2,1)S(1)}, bf16[1,128,1536]{2,1,0:T(8,128)(2,1)}, u32[]{:S(2)}) copy-start(bf16[1,128,1536]{2,1,0:T(8,128)(2,1)} %param.8) | copy-start | bytes 1179652
  71.1 24.7 %copy-start.5 = (bf16[1,128,1536]{2,1,0:T(8,128)(2,1)S(1)}, bf16[1,128,1536]{2,1,0:T(8,128)(2,1)}, u32[]{:S(2)}) copy-start(bf16[1,128,1536]{2,1,0:T(8,128)(2,1)} %param.11) | copy-start | bytes 1179652
  71.1 26.9 %all-to-all-start.1 = ((bf16[2,128,1536]{2,1,0:T(8,128)(2,1)}), bf16[2,128,1536]{2,1,0:T(8,128)(2,1)}, u32[]{:S(2)}, u32[]{:S(2)}) async-start(bf16[2,128,1536]{2,1,0:T(8,128)(2,1)} %bitcast.9), calls=%async_computation.1 | async-start | bytes 1572864 | tf_op jit(solution)/shard_map/all_to_all | solution.py:57
  103.0 0.9 copy-start
  109.9 14.1 %all-to-all-start.2 = ((bf16[2,128,1536]{1,2,0:T(8,128)(2,1)}), bf16[2,128,1536]{1,2,0:T(8,128)(2,1)S(1)}, u32[]{:S(2)}, u32[]{:S(2)}) async-start(bf16[2,128,1536]{1,2,0:T(8,128)(2,1)} %copy.90), calls=%async_computation.2 | async-start | bytes 1572864 | tf_op jit(solution)/shard_map/all_to_all | solution.py:115
  117.7 10.9 %copy-start.1 = (bf16[12,128,256]{2,1,0:T(8,128)(2,1)S(1)}, bf16[12,128,256]{2,1,0:T(8,128)(2,1)}, u32[]{:S(2)}) copy-start(bf16[12,128,256]{2,1,0:T(8,128)(2,1)} %copy-done) | copy-start | bytes 2359300
  124.0 13.2 %all-to-all-start.3 = ((bf16[2,128,1536]{1,2,0:T(8,128)(2,1)}), bf16[2,128,1536]{1,2,0:T(8,128)(2,1)S(1)}, u32[]{:S(2)}, u32[]{:S(2)}) async-start(bf16[2,128,1536]{1,2,0:T(8,128)(2,1)} %copy.92), calls=%async_computation.3 | async-start | bytes 1572864 | tf_op jit(solution)/shard_map/all_to_all | solution.py:122
Sparse Core Ops, SparseCore 0:
  10.3 56.1 all-gather.3
where the time goes:
time: 146 us; the launch traced here: 145 us
  blocking collectives  39.8 us (27%)
  waiting for transfers between devices  38.5 us (26%)
  local copies, waits for them, and re-layouts  17.4 us (12%)
  starting transfers between devices  15.9 us (11%)
  matrix products  15 us (10%)
  between operations  14.2 us (10%)
  other arithmetic  4.45 us (3%)
    all_gather x1, waiting for transfers between devices, local(): lax.all_gather(proj_weight, 'fsdp', axis=0, tiled=True)  29.4 us
    all_gather x1, blocking collectives, local(): value_rows = lax.all_gather(value_states[0], 'ctx', axis=0, tiled=True)  20 us
    all_gather x1, blocking collectives, local(): key_rows = lax.all_gather(key_states[0], 'ctx', axis=0, tiled=True)  19.8 us
    unnamed x24, local copies, waits for them, and re-layouts  6.9 us
    all_to_all x1, waiting for transfers between devices, local(): lax.all_to_all(key_total.astype(jnp.bfloat16).reshape(ctx_count, tok_rows...  6.27 us
    dot_general x1, matrix products, local(): lax.dot_general(grad_slab, lax.all_gather(proj_weight, 'fsdp', axis=0, ti...  4.62 us
    convert_element_type x3, local copies, waits for them, and re-layouts, local(): key_total.astype(jnp.bfloat16).reshape(ctx_count, tok_rows, hid_width)  4.62 us
    all_to_all x1, starting transfers between devices, local(): lax.all_to_all(partial_value.reshape(ctx_count, tok_rows, hid_width), 'ct...  4.44 us
  transfers between devices with their start and end apart: 5, of which 3 were waited for; matrix products, arithmetic and copies ran while one was open for 13% of the time, Pallas kernels for 0%

commit v1 on v0

--- a/solution.py
+++ b/solution.py
@@ -1,6 +1,10 @@
+import functools
+
 import jax
 import jax.numpy as jnp
 from jax import lax
+from jax.experimental import pallas as pl
+from jax.experimental.pallas import tpu as pltpu
 from jax.sharding import PartitionSpec as P
 
 H = 12
@@ -132,6 +136,376 @@
     return (grad_query[None], grad_key[None], grad_value[None])
 
 
+MESH = pl.DeviceIdType.MESH
+CHUNKS = 2
+UP, DOWN, ACROSS, SIBLING = range(4)
+
+
+def dot(a, b, a_dim, b_dim):
+    return lax.dot_general(
+        a, b, (((a_dim,), (b_dim,)), ((), ())), preferred_element_type=jnp.float32
+    )
+
+
+def fused_kernel(
+    q_ref, k_ref, v_ref, o_ref, ln_ref, og_ref, w_ref, mask_ref,
+    gq_ref, gk_ref, gv_ref,
+    wbuf, og_all, q_all, ln_all, p_all, part_own, part_in, grad, dots, dq_out, dq_in,
+    w_send, w_recv, x_send, x_recv,
+):
+    layers = wbuf.shape[0]
+    chunk_rows = wbuf.shape[4]
+    tok = q_ref.shape[1]
+    heads = ln_ref.shape[2]
+    width = w_ref.shape[1]
+    group_width = grad.shape[2]
+    per_group = heads // layers
+    hd = group_width // per_group
+    tile = 2 * tok // mask_ref.shape[3]
+    own_tiles = tok // tile
+    scale = hd ** (-0.5)
+
+    f = lax.axis_index("fsdp")
+    x = lax.axis_index("ctx")
+    core = lax.rem(f, 2)
+    y = lax.rem(lax.div(f, 2), 2)
+    z = lax.div(f, 4)
+    other = 1 - x
+
+    def place(zz, yy, cc):
+        return ((zz * 2 + yy) * 2 + cc, x)
+
+    partner = (f, other)
+    targets = {
+        UP: place(z + 1, y, core),
+        DOWN: place(z - 1, y, core),
+        ACROSS: place(z, 1 - y, core),
+        SIBLING: place(z, y, 1 - core),
+    }
+    has_up = z < layers - 1
+    has_down = z > 0
+
+    barrier = pltpu.get_barrier_semaphore()
+    for device in (partner, targets[ACROSS], targets[SIBLING]):
+        pl.semaphore_signal(barrier, inc=1, device_id=device, device_id_type=MESH)
+
+    @pl.when(has_up)
+    def _():
+        pl.semaphore_signal(barrier, inc=1, device_id=targets[UP], device_id_type=MESH)
+
+    @pl.when(has_down)
+    def _():
+        pl.semaphore_signal(barrier, inc=1, device_id=targets[DOWN], device_id_type=MESH)
+
+    pl.semaphore_wait(barrier, 3 + has_up.astype(jnp.int32) + has_down.astype(jnp.int32))
+
+    def weight_copy(zz, yy, cc, ch, way, own=False):
+        slot = wbuf.at[zz, yy, cc, ch]
+        source = w_ref.at[pl.ds(ch * chunk_rows, chunk_rows)] if own else slot
+        return pltpu.make_async_remote_copy(
+            src_ref=source,
+            dst_ref=slot,
+            send_sem=w_send.at[zz, yy, cc, ch, way],
+            recv_sem=w_recv.at[zz, yy, cc, ch],
+            device_id=targets[way],
+            device_id_type=MESH,
+        )
+
+    def x_copy(source, target, kind, k=0):
+        return pltpu.make_async_remote_copy(
+            src_ref=source,
+            dst_ref=target,
+            send_sem=x_send.at[kind, k],
+            recv_sem=x_recv.at[kind, k],
+            device_id=partner,
+            device_id_type=MESH,
+        )
+
+    og_copy = x_copy(
+        og_ref.at[0, :, pl.ds(pl.multiple_of(other * width, width), width)],
+        og_all.at[pl.ds(tok, tok)],
+        0,
+    )
+    q_copy = x_copy(q_ref.at[0], q_all.at[pl.ds(tok, tok)], 1)
+    ln_copy = x_copy(ln_all.at[0], ln_all.at[1], 2)
+
+    def part_copies(k):
+        return (
+            x_copy(part_own.at[k, pl.ds(tok, tok)], part_in.at[k, pl.ds(0, tok)], 3, k),
+            x_copy(part_own.at[k, pl.ds(0, tok)], part_in.at[k, pl.ds(tok, tok)], 4, k),
+        )
+
+    def dots_copy(k):
+        return x_copy(dots.at[k, 0], dots.at[k, 1], 5, k)
+
+    def dq_copy(k):
+        return x_copy(dq_out.at[k], dq_in.at[k], 6, k)
+
+    def own_weight(action):
+        for ch in range(CHUNKS):
+            for way, there in ((UP, has_up), (DOWN, has_down), (ACROSS, None), (SIBLING, None)):
+                def run(way=way, ch=ch):
+                    action(weight_copy(z, y, core, ch, way, True))
+
+                if there is None:
+                    run()
+                else:
+                    pl.when(there)(run)
+
+    own_weight(lambda copy: copy.start())
+    og_copy.start()
+    ln_all[0] = jnp.zeros(ln_all.shape[1:], ln_all.dtype)
+    ln_all[0, :, pl.ds(0, heads)] = ln_ref[0]
+    ln_copy.start()
+
+    def handle_z(d):
+        for ch in range(CHUNKS):
+
+            @pl.when(z >= d)
+            def _(ch=ch):
+                weight_copy(z - d, y, core, ch, SIBLING).wait_recv()
+
+                @pl.when(has_up)
+                def _():
+                    weight_copy(z - d, y, core, ch, UP).start()
+
+                weight_copy(z - d, y, core, ch, ACROSS).start()
+                weight_copy(z - d, y, core, ch, SIBLING).start()
+
+            @pl.when(z + d < layers)
+            def _(ch=ch):
+                weight_copy(z + d, y, core, ch, SIBLING).wait_recv()
+
+                @pl.when(has_down)
+                def _():
+                    weight_copy(z + d, y, core, ch, DOWN).start()
+
+                weight_copy(z + d, y, core, ch, ACROSS).start()
+                weight_copy(z + d, y, core, ch, SIBLING).start()
+
+    def handle_y(d):
+        for ch in range(CHUNKS):
+
+            @pl.when(z >= d)
+            def _(ch=ch):
+                weight_copy(z - d, 1 - y, core, ch, SIBLING).wait_recv()
+                weight_copy(z - d, 1 - y, core, ch, SIBLING).start()
+
+            if d:
+
+                @pl.when(z + d < layers)
+                def _(ch=ch):
+                    weight_copy(z + d, 1 - y, core, ch, SIBLING).wait_recv()
+                    weight_copy(z + d, 1 - y, core, ch, SIBLING).start()
+
+    def wait_siblings(g):
+        for ch in range(CHUNKS):
+            weight_copy(g, y, 1 - core, ch, SIBLING).wait_recv()
+            weight_copy(g, 1 - y, 1 - core, ch, SIBLING).wait_recv()
+
+    turn = 1 - 2 * lax.div(z, layers // 2)
+
+    def layer(k):
+        return lax.rem(z + turn * k + layers, layers)
+
+    lane_tile = lax.div(lax.broadcasted_iota(jnp.int32, (1, tok), 1), tile)
+
+    def probabilities(b, owner):
+        norm = ln_all[b].astype(jnp.float32)
+        for h in range(heads):
+            cols = pl.ds(h * hd, hd)
+            scores = dot(q_all[pl.ds(b * tok, tok), cols], k_ref[0, :, cols], 1, 1) * scale
+            prob = jnp.exp(scores - norm[:, h : h + 1])
+            for i in range(own_tiles):
+                allowed = jnp.zeros((1, tok), jnp.float32)
+                for j in range(own_tiles):
+                    flag = mask_ref[0, h, owner * own_tiles + i, x * own_tiles + j]
+                    allowed = jnp.where(lane_tile == j, flag.astype(jnp.float32), allowed)
+                p_all[h, pl.ds(b * tok + i * tile, tile), :] = (
+                    prob[i * tile : (i + 1) * tile] * allowed
+                )
+
+    def project(k):
+        g = layer(k)
+        wait_siblings(g)
+        w = wbuf[g].reshape(group_width, width)
+        for b in (1, 0):
+            part = dot(og_all[pl.ds(b * tok, tok)], w, 1, 1)
+            part_own[k, pl.ds(b * tok, tok)] = part.astype(jnp.bfloat16)
+            part_copies(k)[1 - b].start()
+
+    lane = lax.broadcasted_iota(jnp.int32, (tok, dots.shape[3]), 1)
+
+    def reduce(k):
+        g = layer(k)
+        for copy in part_copies(k):
+            copy.wait_recv()
+        total = part_own[k].astype(jnp.float32) + part_in[k].astype(jnp.float32)
+        total = total.astype(jnp.bfloat16)
+        grad[k] = total
+        own = total[:tok].astype(jnp.float32)
+        row = jnp.zeros(lane.shape, jnp.float32)
+        for j in range(per_group):
+            cols = pl.ds(pl.multiple_of((g * per_group + j) * hd, hd), hd)
+            prod = own[:, j * hd : (j + 1) * hd] * o_ref[0, :, cols].astype(jnp.float32)
+            row = jnp.where(lane == j, jnp.sum(prod, axis=1, keepdims=True), row)
+        dots[k, 0] = row.astype(jnp.bfloat16)
+        dots_copy(k).start()
+
+    def attend(k):
+        g = layer(k)
+        dots_copy(k).wait_recv()
+        row = dots[k].reshape(2 * tok, dots.shape[3]).astype(jnp.float32)
+        for j in range(per_group):
+            h = g * per_group + j
+            cols = pl.ds(pl.multiple_of(h * hd, hd), hd)
+            prob = p_all[h]
+            grad_rows = grad[k, :, pl.ds(j * hd, hd)]
+            prob_grad = dot(grad_rows, v_ref[0, :, cols], 1, 1)
+            score_grad = (prob * (prob_grad - row[:, j : j + 1])).astype(jnp.bfloat16)
+            part = dot(score_grad, k_ref[0, :, cols], 1, 0) * scale
+            part = part.astype(jnp.bfloat16)
+            dq_out[k, :, pl.ds(j * hd, hd)] = part[tok:]
+            gq_ref[0, :, cols] = part[:tok]
+            gv_ref[0, :, cols] = dot(prob.astype(jnp.bfloat16), grad_rows, 0, 0).astype(
+                jnp.bfloat16
+            )
+            gk_ref[0, :, cols] = (dot(score_grad, q_all[:, cols], 0, 0) * scale).astype(
+                jnp.bfloat16
+            )
+        dq_copy(k).start()
+
+    def finish(k):
+        g = layer(k)
+        cols = pl.ds(pl.multiple_of(g * group_width, group_width), group_width)
+        dq_copy(k).wait_recv()
+        gq_ref[0, :, cols] = (
+            gq_ref[0, :, cols].astype(jnp.float32) + dq_in[k].astype(jnp.float32)
+        ).astype(jnp.bfloat16)
+
+    for ch in range(CHUNKS):
+        wbuf[z, y, core, ch] = w_ref[pl.ds(ch * chunk_rows, chunk_rows), :]
+    og_all[pl.ds(0, tok)] = og_ref[0, :, pl.ds(pl.multiple_of(x * width, width), width)]
+    q_all[pl.ds(0, tok)] = q_ref[0]
+    handle_y(0)
+    probabilities(0, x)
+    og_copy.wait_recv()
+    q_copy.start()
+    for k in range(layers + 3):
+        if k < layers:
+            if k > 0:
+                handle_y(k)
+            project(k)
+            if k + 1 < layers:
+                handle_z(k + 1)
+        if k == 1:
+            ln_copy.wait_recv()
+            q_copy.wait_recv()
+            probabilities(1, other)
+        if 0 <= k - 1 < layers:
+            reduce(k - 1)
+        if 0 <= k - 2 < layers:
+            attend(k - 2)
+        if 0 <= k - 3 < layers:
+            finish(k - 3)
+
+    own_weight(lambda copy: copy.wait_send())
+    for ch in range(CHUNKS):
+        weight_copy(z, 1 - y, core, ch, SIBLING).wait_send()
+    for d in range(1, layers):
+        for ch in range(CHUNKS):
+
+            @pl.when(z >= d)
+            def _(ch=ch, d=d):
+                @pl.when(has_up)
+                def _():
+                    weight_copy(z - d, y, core, ch, UP).wait_send()
+
+                weight_copy(z - d, y, core, ch, ACROSS).wait_send()
+                weight_copy(z - d, y, core, ch, SIBLING).wait_send()
+                weight_copy(z - d, 1 - y, core, ch, SIBLING).wait_send()
+
+            @pl.when(z + d < layers)
+            def _(ch=ch, d=d):
+                @pl.when(has_down)
+                def _():
+                    weight_copy(z + d, y, core, ch, DOWN).wait_send()
+
+                weight_copy(z + d, y, core, ch, ACROSS).wait_send()
+                weight_copy(z + d, y, core, ch, SIBLING).wait_send()
+                weight_copy(z + d, 1 - y, core, ch, SIBLING).wait_send()
+
+    og_copy.wait_send()
+    q_copy.wait_send()
+    ln_copy.wait_send()
+    for k in range(layers):
+        for copy in part_copies(k):
+            copy.wait_send()
+        dots_copy(k).wait_send()
+        dq_copy(k).wait_send()
+
+
+def fits_kernel(queries, key_states, value_states, attn_out, log_norm, out_grad, proj_weight, tile_mask):
+    fsdp = lax.axis_size("fsdp")
+    heads = log_norm.shape[2]
+    tok = queries.shape[1]
+    rows = proj_weight.shape[0]
+    if lax.axis_size("ctx") != 2 or fsdp % 8 or queries.shape[0] != 1:
+        return False
+    layers = fsdp // 4
+    head_size = queries.shape[2] // heads
+    return (
+        heads % layers == 0
+        and rows % (16 * CHUNKS) == 0
+        and head_size == 128
+        and tok % 128 == 0
+        and tok % (2 * tok // tile_mask.shape[3]) == 0
+        and proj_weight.shape[1] % 128 == 0
+    )
+
+
+def fused(queries, key_states, value_states, attn_out, log_norm, out_grad, proj_weight, tile_mask):
+    layers = lax.axis_size("fsdp") // 4
+    tok, hid = queries.shape[1:]
+    rows, width = proj_weight.shape
+    heads = log_norm.shape[2]
+    group = hid // layers
+    bf16 = jnp.bfloat16
+    whole = pl.BlockSpec(memory_space=pltpu.VMEM)
+    return tuple(pl.pallas_call(
+        fused_kernel,
+        out_shape=[jax.ShapeDtypeStruct(queries.shape, bf16)] * 3,
+        in_specs=[whole] * 7 + [pl.BlockSpec(memory_space=pltpu.SMEM)],
+        out_specs=[whole] * 3,
+        scratch_shapes=[
+            pltpu.VMEM((layers, 2, 2, CHUNKS, rows // CHUNKS, width), bf16),
+            pltpu.VMEM((2 * tok, width), bf16),
+            pltpu.VMEM((2 * tok, hid), bf16),
+            pltpu.VMEM((2, tok, 128), bf16),
+            pltpu.VMEM((heads, 2 * tok, tok), jnp.float32),
+            pltpu.VMEM((layers, 2 * tok, group), bf16),
+            pltpu.VMEM((layers, 2 * tok, group), bf16),
+            pltpu.VMEM((layers, 2 * tok, group), bf16),
+            pltpu.VMEM((layers, 2, tok, 128), bf16),
+            pltpu.VMEM((layers, tok, group), bf16),
+            pltpu.VMEM((layers, tok, group), bf16),
+            pltpu.SemaphoreType.DMA((layers, 2, 2, CHUNKS, 4)),
+            pltpu.SemaphoreType.DMA((layers, 2, 2, CHUNKS)),
+            pltpu.SemaphoreType.DMA((7, layers)),
+            pltpu.SemaphoreType.DMA((7, layers)),
+        ],
+        compiler_params=pltpu.CompilerParams(
+            collective_id=0, has_side_effects=True, vmem_limit_bytes=40 * 1024 * 1024
+        ),
+    )(queries, key_states, value_states, attn_out, log_norm, out_grad, proj_weight, tile_mask))
+
+
+def plan(*arrays):
+    if fits_kernel(*arrays):
+        return fused(*arrays)
+    return local(*arrays)
+
+
 def solution(mesh):
     placed = (
         P("fsdp", "ctx", None),
@@ -144,7 +518,7 @@
         P("fsdp", None, None, None),
     )
     return jax.shard_map(
-        local,
+        plan,
         mesh=mesh,
         in_specs=placed,
         out_specs=(P("fsdp", "ctx", None), P("fsdp", "ctx", None), P("fsdp", "ctx", None)),

time: 146 us -> 73.9 us (0.51)
  Pallas kernels: 0 us -> 63.5 us
  blocking collectives: 39.8 us -> 0 us
  waiting for transfers between devices: 38.5 us -> 0 us
  starting transfers between devices: 15.9 us -> 0 us
  matrix products: 15 us -> 0 us
  between operations: 14.2 us -> 0.66 us
  local copies, waits for them, and re-layouts: 17.4 us -> 9.26 us
  other arithmetic: 4.45 us -> 0 us
    pallas_call x0 -> x1, Pallas kernels: none -> 63.5 us  [fused(): pl.pallas_call(fused_kernel, out_shape=[jax.ShapeDtypeStruct(queries.shap...]
    all_gather x2 -> x0, blocking collectives: 39.8 us -> none  [the longest x1 20 us: local(): value_rows = lax.all_gather(value_states[0], 'ctx', axis=0, tiled=True)]
    all_gather x1 -> x0, waiting for transfers between devices: 29.4 us -> none  [local(): lax.all_gather(proj_weight, 'fsdp', axis=0, tiled=True)]
    all_to_all x4 -> x0, starting transfers between devices: 15.8 us -> none  [the longest x1 4.44 us: local(): lax.all_to_all(partial_value.reshape(ctx_count, tok_rows, hid_width), 'ct...]
    dot_general x7 -> x0, matrix products: 15 us -> none  [the longest x1 4.62 us: local(): lax.dot_general(grad_slab, lax.all_gather(proj_weight, 'fsdp', axis=0, ti...]
    all_to_all x4 -> x0, waiting for transfers between devices: 8.45 us -> none  [the longest x1 6.27 us: local(): lax.all_to_all(key_total.astype(jnp.bfloat16).reshape(ctx_count, tok_rows...]
    convert_element_type x6 -> x0, local copies, waits for them, and re-layouts: 7.76 us -> none  [the longest x3 4.62 us: local(): key_total.astype(jnp.bfloat16).reshape(ctx_count, tok_rows, hid_width)]
    reduce_sum x5 -> x0, other arithmetic: 4.43 us -> none  [the longest x1 2.11 us: local(): jnp.sum(arrived.astype(jnp.float32), axis=0).astype(jnp.bfloat16)]
  transfers between devices with their start and end apart: 5 -> 0, of which waited for: 3 -> 0; matrix products, arithmetic and copies ran while one was open for 13% -> 0% of each run, Pallas kernels for 0% -> 0%
where the time goes in v1:
time: 73.9 us; the launch traced here: 73.5 us
  Pallas kernels  63.5 us (86%)
  local copies, waits for them, and re-layouts  9.26 us (13%)
    pallas_call x1, Pallas kernels, fused(): pl.pallas_call(fused_kernel, out_shape=[jax.ShapeDtypeStruct(queries.shap...  63.5 us
    unnamed x19, local copies, waits for them, and re-layouts  9.26 us

profile of v1, /device:TPU:0, one launch (start us, length us, event | category | flops | bytes accessed | tf_op | source)
XLA Modules:
  0.0 73.5 jit_solution(11056844895314081277)
XLA Ops:
  0.6 0.0 copy-start.6
  0.6 0.8 %copy.12.mask_ref = s32[1,12,4,4]{3,2,1,0:T(4,128)S(1)} copy(s32[1,12,4,4]{1,3,2,0:T(4,128)} %param.15) | data formatting | bytes 1536 | tf_op args[7]
  1.4 0.0 copy-done.6
  1.5 0.1 copy.11.ln_ref
  1.6 0.0 copy-start
  1.6 1.1 %copy-done = bf16[1,128,3072]{2,1,0:T(8,128)(2,1)S(1)} copy-done((bf16[1,128,3072]{2,1,0:T(8,128)(2,1)S(1)}, bf16[1,128,3072]{2,1,0:T(8,128)(2,1)}, u32[]{:S(2)}) %copy-start) | copy-done | bytes 786456
  2.7 0.0 copy-start.1
  2.7 1.0 %copy-done.1 = bf16[1,128,1536]{2,1,0:T(8,128)(2,1)S(1)} copy-done((bf16[1,128,1536]{2,1,0:T(8,128)(2,1)S(1)}, bf16[1,128,1536]{2,1,0:T(8,128)(2,1)}, u32[]{:S(2)}) %copy-start.1) | copy-done | bytes 393240
  3.7 0.0 copy-start.2
  3.7 1.0 %copy-done.2 = bf16[1,128,1536]{2,1,0:T(8,128)(2,1)S(1)} copy-done((bf16[1,128,1536]{2,1,0:T(8,128)(2,1)S(1)}, bf16[1,128,1536]{2,1,0:T(8,128)(2,1)}, u32[]{:S(2)}) %copy-start.2) | copy-done | bytes 393240
  4.7 0.0 copy-start.3
  4.7 1.0 %copy-done.3 = bf16[1,128,1536]{2,1,0:T(8,128)(2,1)S(1)} copy-done((bf16[1,128,1536]{2,1,0:T(8,128)(2,1)S(1)}, bf16[1,128,1536]{2,1,0:T(8,128)(2,1)}, u32[]{:S(2)}) %copy-start.3) | copy-done | bytes 393240
  5.7 0.0 copy-start.4
  5.7 1.0 %copy-done.4 = bf16[1,128,1536]{2,1,0:T(8,128)(2,1)S(1)} copy-done((bf16[1,128,1536]{2,1,0:T(8,128)(2,1)S(1)}, bf16[1,128,1536]{2,1,0:T(8,128)(2,1)}, u32[]{:S(2)}) %copy-start.4) | copy-done | bytes 393240
  6.7 0.0 copy-start.5
  6.7 1.0 %copy-done.5 = bf16[96,1536]{1,0:T(8,128)(2,1)S(1)} copy-done((bf16[96,1536]{1,0:T(8,128)(2,1)S(1)}, bf16[96,1536]{1,0:T(8,128)(2,1)}, u32[]{:S(2)}) %copy-start.5) | copy-done | bytes 294936
  7.7 63.5 %shard_map.103 = (bf16[1,128,1536]{2,1,0:T(8,128)(2,1)S(1)}, bf16[1,128,1536]{2,1,0:T(8,128)(2,1)S(1)}, bf16[1,128,1536]{2,1,0:T(8,128)(2,1)S(1)}) custom-call(bf16[1,128,1536]{2,1,0:T(8,128)(2,1)S(1)} %copy-done.1, bf16[1,128,1536]{2,1,0:T(8,128)(2,1)S(1)} %copy-done.2, bf16[1,128,1536]{2,1,0:T(8,128)(2,1)S(1)} %copy-done.3, ...), custom_call_target="tpu_custom_call" | custom-call | tf_op jit(solution)/shard_map/pallas_call | solution.py:475
  71.2 0.7 %copy.16 = bf16[1,128,1536]{2,1,0:T(8,128)(2,1)} copy(bf16[1,128,1536]{2,1,0:T(8,128)(2,1)S(1)} %get-tuple-element.6) | data formatting | bytes 786432
  72.0 0.7 %copy.17 = bf16[1,128,1536]{2,1,0:T(8,128)(2,1)} copy(bf16[1,128,1536]{2,1,0:T(8,128)(2,1)S(1)} %get-tuple-element.7) | data formatting | bytes 786432
  72.7 0.7 %copy.18 = bf16[1,128,1536]{2,1,0:T(8,128)(2,1)} copy(bf16[1,128,1536]{2,1,0:T(8,128)(2,1)S(1)} %get-tuple-element.8) | data formatting | bytes 786432
Async XLA Ops:
  0.6 0.8 %copy-start.6 = (bf16[1,128,12]{1,2,0:T(8,128)(2,1)S(1)}, bf16[1,128,12]{1,2,0:T(8,128)(2,1)}, u32[]{:S(2)}) copy-start(bf16[1,128,12]{1,2,0:T(8,128)(2,1)} %param.12) | copy-start | bytes 9220
  1.6 1.1 %copy-start = (bf16[1,128,3072]{2,1,0:T(8,128)(2,1)S(1)}, bf16[1,128,3072]{2,1,0:T(8,128)(2,1)}, u32[]{:S(2)}) copy-start(bf16[1,128,3072]{2,1,0:T(8,128)(2,1)} %og_ref.1) | copy-start | bytes 2359300
  2.7 1.0 %copy-start.1 = (bf16[1,128,1536]{2,1,0:T(8,128)(2,1)S(1)}, bf16[1,128,1536]{2,1,0:T(8,128)(2,1)}, u32[]{:S(2)}) copy-start(bf16[1,128,1536]{2,1,0:T(8,128)(2,1)} %q_ref.1) | copy-start | bytes 1179652
  3.7 1.0 %copy-start.2 = (bf16[1,128,1536]{2,1,0:T(8,128)(2,1)S(1)}, bf16[1,128,1536]{2,1,0:T(8,128)(2,1)}, u32[]{:S(2)}) copy-start(bf16[1,128,1536]{2,1,0:T(8,128)(2,1)} %k_ref.1) | copy-start | bytes 1179652
  4.7 1.0 %copy-start.3 = (bf16[1,128,1536]{2,1,0:T(8,128)(2,1)S(1)}, bf16[1,128,1536]{2,1,0:T(8,128)(2,1)}, u32[]{:S(2)}) copy-start(bf16[1,128,1536]{2,1,0:T(8,128)(2,1)} %v_ref.1) | copy-start | bytes 1179652
  5.7 1.0 %copy-start.4 = (bf16[1,128,1536]{2,1,0:T(8,128)(2,1)S(1)}, bf16[1,128,1536]{2,1,0:T(8,128)(2,1)}, u32[]{:S(2)}) copy-start(bf16[1,128,1536]{2,1,0:T(8,128)(2,1)} %o_ref.1) | copy-start | bytes 1179652
  6.7 1.0 %copy-start.5 = (bf16[96,1536]{1,0:T(8,128)(2,1)S(1)}, bf16[96,1536]{1,0:T(8,128)(2,1)}, u32[]{:S(2)}) copy-start(bf16[96,1536]{1,0:T(8,128)(2,1)} %w_ref.1) | copy-start | bytes 884740

commit v2 on v1

--- a/solution.py
+++ b/solution.py
@@ -150,18 +150,19 @@
 def fused_kernel(
     q_ref, k_ref, v_ref, o_ref, ln_ref, og_ref, w_ref, mask_ref,
     gq_ref, gk_ref, gv_ref,
-    wbuf, og_all, q_all, ln_all, p_all, part_own, part_in, grad, dots, dq_out, dq_in,
-    w_send, w_recv, x_send, x_recv,
+    wbuf, og_all, q_all, k_all, v_all, o_all, ln_all, p_all,
+    part_own, part_in, grad, dots, dq_out, dq_in,
+    w_send, w_recv, x_send, x_recv, local_sem,
 ):
     layers = wbuf.shape[0]
-    chunk_rows = wbuf.shape[4]
+    chunk_rows = wbuf.shape[3] // CHUNKS
     tok = q_ref.shape[1]
     heads = ln_ref.shape[2]
     width = w_ref.shape[1]
     group_width = grad.shape[2]
     per_group = heads // layers
     hd = group_width // per_group
-    tile = 2 * tok // mask_ref.shape[3]
+    tile = 2 * tok // mask_ref.shape[2]
     own_tiles = tok // tile
     scale = hd ** (-0.5)
 
@@ -185,6 +186,23 @@
     has_up = z < layers - 1
     has_down = z > 0
 
+    own_block = pl.ds(pl.multiple_of(x * width, width), width)
+    load_w, load_og, load_q, load_k, load_v, load_o = (
+        pltpu.make_async_copy(source, target, local_sem.at[n])
+        for n, (source, target) in enumerate(
+            (
+                (w_ref, wbuf.at[z, y, core]),
+                (og_ref.at[0, :, own_block], og_all.at[pl.ds(0, tok)]),
+                (q_ref.at[0], q_all.at[pl.ds(0, tok)]),
+                (k_ref.at[0], k_all),
+                (v_ref.at[0], v_all),
+                (o_ref.at[0], o_all),
+            )
+        )
+    )
+    for load in (load_q, load_k, load_og, load_w, load_v, load_o):
+        load.start()
+
     barrier = pltpu.get_barrier_semaphore()
     for device in (partner, targets[ACROSS], targets[SIBLING]):
         pl.semaphore_signal(barrier, inc=1, device_id=device, device_id_type=MESH)
@@ -200,8 +218,9 @@
     pl.semaphore_wait(barrier, 3 + has_up.astype(jnp.int32) + has_down.astype(jnp.int32))
 
     def weight_copy(zz, yy, cc, ch, way, own=False):
-        slot = wbuf.at[zz, yy, cc, ch]
-        source = w_ref.at[pl.ds(ch * chunk_rows, chunk_rows)] if own else slot
+        rows = pl.ds(ch * chunk_rows, chunk_rows)
+        slot = wbuf.at[zz, yy, cc, rows]
+        source = w_ref.at[rows] if own else slot
         return pltpu.make_async_remote_copy(
             src_ref=source,
             dst_ref=slot,
@@ -314,12 +333,12 @@
         norm = ln_all[b].astype(jnp.float32)
         for h in range(heads):
             cols = pl.ds(h * hd, hd)
-            scores = dot(q_all[pl.ds(b * tok, tok), cols], k_ref[0, :, cols], 1, 1) * scale
+            scores = dot(q_all[pl.ds(b * tok, tok), cols], k_all[:, cols], 1, 1) * scale
             prob = jnp.exp(scores - norm[:, h : h + 1])
             for i in range(own_tiles):
                 allowed = jnp.zeros((1, tok), jnp.float32)
                 for j in range(own_tiles):
-                    flag = mask_ref[0, h, owner * own_tiles + i, x * own_tiles + j]
+                    flag = mask_ref[0, owner * own_tiles + i, x * own_tiles + j, h]
                     allowed = jnp.where(lane_tile == j, flag.astype(jnp.float32), allowed)
                 p_all[h, pl.ds(b * tok + i * tile, tile), :] = (
                     prob[i * tile : (i + 1) * tile] * allowed
@@ -347,7 +366,7 @@
         row = jnp.zeros(lane.shape, jnp.float32)
         for j in range(per_group):
             cols = pl.ds(pl.multiple_of((g * per_group + j) * hd, hd), hd)
-            prod = own[:, j * hd : (j + 1) * hd] * o_ref[0, :, cols].astype(jnp.float32)
+            prod = own[:, j * hd : (j + 1) * hd] * o_all[:, cols].astype(jnp.float32)
             row = jnp.where(lane == j, jnp.sum(prod, axis=1, keepdims=True), row)
         dots[k, 0] = row.astype(jnp.bfloat16)
         dots_copy(k).start()
@@ -361,9 +380,9 @@
             cols = pl.ds(pl.multiple_of(h * hd, hd), hd)
             prob = p_all[h]
             grad_rows = grad[k, :, pl.ds(j * hd, hd)]
-            prob_grad = dot(grad_rows, v_ref[0, :, cols], 1, 1)
+            prob_grad = dot(grad_rows, v_all[:, cols], 1, 1)
             score_grad = (prob * (prob_grad - row[:, j : j + 1])).astype(jnp.bfloat16)
-            part = dot(score_grad, k_ref[0, :, cols], 1, 0) * scale
+            part = dot(score_grad, k_all[:, cols], 1, 0) * scale
             part = part.astype(jnp.bfloat16)
             dq_out[k, :, pl.ds(j * hd, hd)] = part[tok:]
             gq_ref[0, :, cols] = part[:tok]
@@ -383,25 +402,29 @@
             gq_ref[0, :, cols].astype(jnp.float32) + dq_in[k].astype(jnp.float32)
         ).astype(jnp.bfloat16)
 
-    for ch in range(CHUNKS):
-        wbuf[z, y, core, ch] = w_ref[pl.ds(ch * chunk_rows, chunk_rows), :]
-    og_all[pl.ds(0, tok)] = og_ref[0, :, pl.ds(pl.multiple_of(x * width, width), width)]
-    q_all[pl.ds(0, tok)] = q_ref[0]
+    handle_z(1)
     handle_y(0)
+    load_q.wait()
+    load_k.wait()
     probabilities(0, x)
     og_copy.wait_recv()
     q_copy.start()
+    load_og.wait()
+    load_w.wait()
     for k in range(layers + 3):
         if k < layers:
-            if k > 0:
-                handle_y(k)
             project(k)
+            if k + 2 < layers:
+                handle_z(k + 2)
             if k + 1 < layers:
-                handle_z(k + 1)
+                handle_y(k + 1)
         if k == 1:
             ln_copy.wait_recv()
             q_copy.wait_recv()
             probabilities(1, other)
+            load_v.wait()
+        if k == 0:
+            load_o.wait()
         if 0 <= k - 1 < layers:
             reduce(k - 1)
         if 0 <= k - 2 < layers:
@@ -472,15 +495,20 @@
     group = hid // layers
     bf16 = jnp.bfloat16
     whole = pl.BlockSpec(memory_space=pltpu.VMEM)
+    far = pl.BlockSpec(memory_space=pl.ANY)
+    mask = jnp.transpose(tile_mask, (0, 2, 3, 1))
     return tuple(pl.pallas_call(
         fused_kernel,
         out_shape=[jax.ShapeDtypeStruct(queries.shape, bf16)] * 3,
-        in_specs=[whole] * 7 + [pl.BlockSpec(memory_space=pltpu.SMEM)],
+        in_specs=[far] * 4 + [whole] + [far] * 2 + [pl.BlockSpec(memory_space=pltpu.SMEM)],
         out_specs=[whole] * 3,
         scratch_shapes=[
-            pltpu.VMEM((layers, 2, 2, CHUNKS, rows // CHUNKS, width), bf16),
+            pltpu.VMEM((layers, 2, 2, rows, width), bf16),
             pltpu.VMEM((2 * tok, width), bf16),
             pltpu.VMEM((2 * tok, hid), bf16),
+            pltpu.VMEM((tok, hid), bf16),
+            pltpu.VMEM((tok, hid), bf16),
+            pltpu.VMEM((tok, hid), bf16),
             pltpu.VMEM((2, tok, 128), bf16),
             pltpu.VMEM((heads, 2 * tok, tok), jnp.float32),
             pltpu.VMEM((layers, 2 * tok, group), bf16),
@@ -493,11 +521,12 @@
             pltpu.SemaphoreType.DMA((layers, 2, 2, CHUNKS)),
             pltpu.SemaphoreType.DMA((7, layers)),
             pltpu.SemaphoreType.DMA((7, layers)),
+            pltpu.SemaphoreType.DMA((6,)),
         ],
         compiler_params=pltpu.CompilerParams(
-            collective_id=0, has_side_effects=True, vmem_limit_bytes=40 * 1024 * 1024
+            collective_id=0, has_side_effects=True, vmem_limit_bytes=56 * 1024 * 1024
         ),
-    )(queries, key_states, value_states, attn_out, log_norm, out_grad, proj_weight, tile_mask))
+    )(queries, key_states, value_states, attn_out, log_norm, out_grad, proj_weight, mask))
 
 
 def plan(*arrays):

time: 73.9 us -> 63.2 us (0.86)
  Pallas kernels: 63.5 us -> 57.2 us
  local copies, waits for them, and re-layouts: 9.26 us -> 5.12 us
    pallas_call x1, Pallas kernels: 63.5 us -> 57.2 us  [fused(): pl.pallas_call(fused_kernel, out_shape=[jax.ShapeDtypeStruct(queries.shap...]
    unnamed x19 -> x8, local copies, waits for them, and re-layouts: 9.26 us -> 5.12 us
where the time goes in v2:
time: 63.2 us; the launch traced here: 62.9 us
  Pallas kernels  57.2 us (91%)
  local copies, waits for them, and re-layouts  5.12 us (8%)
  between operations  0.65 us (1%)
    pallas_call x1, Pallas kernels, fused(): pl.pallas_call(fused_kernel, out_shape=[jax.ShapeDtypeStruct(queries.shap...  57.2 us
    unnamed x8, local copies, waits for them, and re-layouts  5.12 us

profile of v2, /device:TPU:0, one launch (start us, length us, event | category | flops | bytes accessed | tf_op | source)
XLA Modules:
  0.0 62.9 jit_solution(15409596692591521719)
XLA Ops:
  0.6 1.4 %copy.11.ln_ref = bf16[1,128,12]{2,1,0:T(8,128)(2,1)} copy(bf16[1,128,12]{1,2,0:T(8,128)(2,1)} %param.12) | data formatting | bytes 6144 | tf_op args[4]
  2.0 57.2 %shard_map.103 = (bf16[1,128,1536]{2,1,0:T(8,128)(2,1)}, bf16[1,128,1536]{2,1,0:T(8,128)(2,1)}, bf16[1,128,1536]{2,1,0:T(8,128)(2,1)}) custom-call(bf16[1,128,1536]{2,1,0:T(8,128)(2,1)} %q_ref.1, bf16[1,128,1536]{2,1,0:T(8,128)(2,1)} %k_ref.1, bf16[1,128,1536]{2,1,0:T(8,128)(2,1)} %v_ref.1, bf16[1,128,1536]{2,1,0:T(8,128)(2,1)} %o_ref.1, ...), custom_call_target="tpu_custom_call" | custom-call | tf_op jit(solution)/shard_map/pallas_call | solution.py:500
  59.2 0.0 copy-start.1
  59.2 1.8 %copy.15 = bf16[1,128,1536]{2,1,0:T(8,128)(2,1)} copy(bf16[1,128,1536]{2,1,0:T(8,128)(2,1)} %get-tuple-element.6) | data formatting | bytes 786432
  61.1 0.0 copy-done.1
  61.1 0.0 copy-start
  61.1 0.7 %copy.16 = bf16[1,128,1536]{2,1,0:T(8,128)(2,1)} copy(bf16[1,128,1536]{2,1,0:T(8,128)(2,1)S(1)} %copy-done.1) | data formatting | bytes 786432
  61.8 0.4 copy-done
  62.2 0.7 %copy.17 = bf16[1,128,1536]{2,1,0:T(8,128)(2,1)} copy(bf16[1,128,1536]{2,1,0:T(8,128)(2,1)S(1)} %copy-done) | data formatting | bytes 786432
Async XLA Ops:
  59.2 1.8 %copy-start.1 = (bf16[1,128,1536]{2,1,0:T(8,128)(2,1)S(1)}, bf16[1,128,1536]{2,1,0:T(8,128)(2,1)}, u32[]{:S(2)}) copy-start(bf16[1,128,1536]{2,1,0:T(8,128)(2,1)} %get-tuple-element.7) | copy-start | bytes 1179652
  61.1 1.1 %copy-start = (bf16[1,128,1536]{2,1,0:T(8,128)(2,1)S(1)}, bf16[1,128,1536]{2,1,0:T(8,128)(2,1)}, u32[]{:S(2)}) copy-start(bf16[1,128,1536]{2,1,0:T(8,128)(2,1)} %get-tuple-element.8) | copy-start | bytes 1179652

commit v3 on v2

--- a/solution.py
+++ b/solution.py
@@ -137,7 +137,7 @@
 
 
 MESH = pl.DeviceIdType.MESH
-CHUNKS = 2
+CHUNKS = 1
 UP, DOWN, ACROSS, SIBLING = range(4)
 
 
@@ -157,7 +157,7 @@
     layers = wbuf.shape[0]
     chunk_rows = wbuf.shape[3] // CHUNKS
     tok = q_ref.shape[1]
-    heads = ln_ref.shape[2]
+    heads = ln_ref.shape[1]
     width = w_ref.shape[1]
     group_width = grad.shape[2]
     per_group = heads // layers
@@ -274,7 +274,7 @@
     own_weight(lambda copy: copy.start())
     og_copy.start()
     ln_all[0] = jnp.zeros(ln_all.shape[1:], ln_all.dtype)
-    ln_all[0, :, pl.ds(0, heads)] = ln_ref[0]
+    ln_all[0, pl.ds(0, heads), :] = ln_ref[0]
     ln_copy.start()
 
     def handle_z(d):
@@ -327,14 +327,18 @@
     def layer(k):
         return lax.rem(z + turn * k + layers, layers)
 
+    def spread(rows, h):
+        pick = lax.broadcasted_iota(jnp.int32, (rows.shape[0], hd), 0) == h
+        return dot(rows, jnp.where(pick, 1.0, 0.0).astype(jnp.bfloat16), 0, 0)
+
     lane_tile = lax.div(lax.broadcasted_iota(jnp.int32, (1, tok), 1), tile)
 
     def probabilities(b, owner):
-        norm = ln_all[b].astype(jnp.float32)
+        norm = ln_all[b]
         for h in range(heads):
             cols = pl.ds(h * hd, hd)
             scores = dot(q_all[pl.ds(b * tok, tok), cols], k_all[:, cols], 1, 1) * scale
-            prob = jnp.exp(scores - norm[:, h : h + 1])
+            prob = jnp.exp(scores - spread(norm, h))
             for i in range(own_tiles):
                 allowed = jnp.zeros((1, tok), jnp.float32)
                 for j in range(own_tiles):
@@ -353,7 +357,7 @@
             part_own[k, pl.ds(b * tok, tok)] = part.astype(jnp.bfloat16)
             part_copies(k)[1 - b].start()
 
-    lane = lax.broadcasted_iota(jnp.int32, (tok, dots.shape[3]), 1)
+    lane = lax.broadcasted_iota(jnp.int32, (tok, hd), 1)
 
     def reduce(k):
         g = layer(k)
@@ -368,20 +372,20 @@
             cols = pl.ds(pl.multiple_of((g * per_group + j) * hd, hd), hd)
             prod = own[:, j * hd : (j + 1) * hd] * o_all[:, cols].astype(jnp.float32)
             row = jnp.where(lane == j, jnp.sum(prod, axis=1, keepdims=True), row)
-        dots[k, 0] = row.astype(jnp.bfloat16)
+        dots[k, 0] = jnp.transpose(row)[: dots.shape[2]].astype(jnp.bfloat16)
         dots_copy(k).start()
 
     def attend(k):
         g = layer(k)
         dots_copy(k).wait_recv()
-        row = dots[k].reshape(2 * tok, dots.shape[3]).astype(jnp.float32)
         for j in range(per_group):
             h = g * per_group + j
             cols = pl.ds(pl.multiple_of(h * hd, hd), hd)
             prob = p_all[h]
             grad_rows = grad[k, :, pl.ds(j * hd, hd)]
             prob_grad = dot(grad_rows, v_all[:, cols], 1, 1)
-            score_grad = (prob * (prob_grad - row[:, j : j + 1])).astype(jnp.bfloat16)
+            row = jnp.concatenate([spread(dots[k, 0], j), spread(dots[k, 1], j)], axis=0)
+            score_grad = (prob * (prob_grad - row)).astype(jnp.bfloat16)
             part = dot(score_grad, k_all[:, cols], 1, 0) * scale
             part = part.astype(jnp.bfloat16)
             dq_out[k, :, pl.ds(j * hd, hd)] = part[tok:]
@@ -418,7 +422,7 @@
                 handle_z(k + 2)
             if k + 1 < layers:
                 handle_y(k + 1)
-        if k == 1:
+        if k == 2:
             ln_copy.wait_recv()
             q_copy.wait_recv()
             probabilities(1, other)
@@ -473,12 +477,14 @@
     heads = log_norm.shape[2]
     tok = queries.shape[1]
     rows = proj_weight.shape[0]
-    if lax.axis_size("ctx") != 2 or fsdp % 8 or queries.shape[0] != 1:
+    if lax.axis_size("ctx") != 2 or fsdp % 8 or fsdp < 12 or queries.shape[0] != 1:
         return False
     layers = fsdp // 4
     head_size = queries.shape[2] // heads
     return (
         heads % layers == 0
+        and heads <= 16
+        and tok == head_size
         and rows % (16 * CHUNKS) == 0
         and head_size == 128
         and tok % 128 == 0
@@ -492,6 +498,7 @@
     tok, hid = queries.shape[1:]
     rows, width = proj_weight.shape
     heads = log_norm.shape[2]
+    norm = jnp.transpose(log_norm, (0, 2, 1))
     group = hid // layers
     bf16 = jnp.bfloat16
     whole = pl.BlockSpec(memory_space=pltpu.VMEM)
@@ -509,12 +516,12 @@
             pltpu.VMEM((tok, hid), bf16),
             pltpu.VMEM((tok, hid), bf16),
             pltpu.VMEM((tok, hid), bf16),
-            pltpu.VMEM((2, tok, 128), bf16),
+            pltpu.VMEM((2, 16, tok), bf16),
             pltpu.VMEM((heads, 2 * tok, tok), jnp.float32),
             pltpu.VMEM((layers, 2 * tok, group), bf16),
             pltpu.VMEM((layers, 2 * tok, group), bf16),
             pltpu.VMEM((layers, 2 * tok, group), bf16),
-            pltpu.VMEM((layers, 2, tok, 128), bf16),
+            pltpu.VMEM((layers, 2, 16, tok), bf16),
             pltpu.VMEM((layers, tok, group), bf16),
             pltpu.VMEM((layers, tok, group), bf16),
             pltpu.SemaphoreType.DMA((layers, 2, 2, CHUNKS, 4)),
@@ -526,7 +533,7 @@
         compiler_params=pltpu.CompilerParams(
             collective_id=0, has_side_effects=True, vmem_limit_bytes=56 * 1024 * 1024
         ),
-    )(queries, key_states, value_states, attn_out, log_norm, out_grad, proj_weight, mask))
+    )(queries, key_states, value_states, attn_out, norm, out_grad, proj_weight, mask))
 
 
 def plan(*arrays):

time: 63.2 us -> 59.8 us (0.946)
  Pallas kernels: 57.2 us -> 55.2 us
  local copies, waits for them, and re-layouts: 5.12 us -> 3.7 us
    pallas_call x1, Pallas kernels: 57.2 us -> 55.2 us  [fused(): pl.pallas_call(fused_kernel, out_shape=[jax.ShapeDtypeStruct(queries.shap...]
    unnamed x8 -> x7, local copies, waits for them, and re-layouts: 5.12 us -> 3.7 us
where the time goes in v3:
time: 59.8 us; the launch traced here: 59.5 us
  Pallas kernels  55.2 us (92%)
  local copies, waits for them, and re-layouts  3.7 us (6%)
  between operations  0.65 us (1%)
    pallas_call x1, Pallas kernels, fused(): pl.pallas_call(fused_kernel, out_shape=[jax.ShapeDtypeStruct(queries.shap...  55.2 us
    unnamed x7, local copies, waits for them, and re-layouts  3.7 us

profile of v3, /device:TPU:0, one launch (start us, length us, event | category | flops | bytes accessed | tf_op | source)
XLA Modules:
  0.0 59.5 jit_solution(16897585946522017603)
XLA Ops:
  0.6 55.2 %shard_map.103 = (bf16[1,128,1536]{2,1,0:T(8,128)(2,1)}, bf16[1,128,1536]{2,1,0:T(8,128)(2,1)}, bf16[1,128,1536]{2,1,0:T(8,128)(2,1)}) custom-call(bf16[1,128,1536]{2,1,0:T(8,128)(2,1)} %q_ref.1, bf16[1,128,1536]{2,1,0:T(8,128)(2,1)} %k_ref.1, bf16[1,128,1536]{2,1,0:T(8,128)(2,1)} %v_ref.1, bf16[1,128,1536]{2,1,0:T(8,128)(2,1)} %o_ref.1, ...), custom_call_target="tpu_custom_call" | custom-call | tf_op jit(solution)/shard_map/pallas_call | solution.py:507
  55.8 0.0 copy-start.1
  55.8 1.8 %copy.14 = bf16[1,128,1536]{2,1,0:T(8,128)(2,1)} copy(bf16[1,128,1536]{2,1,0:T(8,128)(2,1)} %get-tuple-element.6) | data formatting | bytes 786432
  57.6 0.0 copy-done.1
  57.6 0.0 copy-start
  57.6 0.7 %copy.15 = bf16[1,128,1536]{2,1,0:T(8,128)(2,1)} copy(bf16[1,128,1536]{2,1,0:T(8,128)(2,1)S(1)} %copy-done.1) | data formatting | bytes 786432
  58.4 0.4 copy-done
  58.8 0.7 %copy.16 = bf16[1,128,1536]{2,1,0:T(8,128)(2,1)} copy(bf16[1,128,1536]{2,1,0:T(8,128)(2,1)S(1)} %copy-done) | data formatting | bytes 786432
Async XLA Ops:
  55.8 1.8 %copy-start.1 = (bf16[1,128,1536]{2,1,0:T(8,128)(2,1)S(1)}, bf16[1,128,1536]{2,1,0:T(8,128)(2,1)}, u32[]{:S(2)}) copy-start(bf16[1,128,1536]{2,1,0:T(8,128)(2,1)} %get-tuple-element.7) | copy-start | bytes 1179652
  57.6 1.1 %copy-start = (bf16[1,128,1536]{2,1,0:T(8,128)(2,1)S(1)}, bf16[1,128,1536]{2,1,0:T(8,128)(2,1)}, u32[]{:S(2)}) copy-start(bf16[1,128,1536]{2,1,0:T(8,128)(2,1)} %get-tuple-element.8) | copy-start | bytes 1179652
